TPU v7x, 128 devices: a whole 4x4x4 slice. The times are simulated.
128 devices in a mesh: head: 4 (over z_hi, core), freq: 32 (over y, x, z_lo).
Axes of the slice: x: 4, y: 4, z: 4 (z_hi: 2, z_lo: 2; z = z_hi * 2 + z_lo), core: 2. Of those that a mesh axis runs over, the one named last changes fastest.
Arguments:
- transfer: bfloat16 [2, 36, 256, 65536], P(None, 'head', None, 'freq'), may hold values from -6 to 6
- amplitudes: float32 [2, 36, 65536], P(None, 'head', 'freq'), may hold values from -0.00390625 to 0.00390625
- weights: float32 [36], P('head'), may hold values from 0.2 to 2
Outputs:
- stress: float32 [256, 256, 256], P('head', 'freq')
All inputs are finite; a program needn't handle non-finite values.
Results may differ from a plain program's by a relative error of at most 0.0036.
Values may be sent and summed in bfloat16 or wider, within the bound.
A program may use at most 128 MiB of HBM per device.

v0:
```python
import math

import jax
import jax.numpy as jnp
from jax import lax
from jax.sharding import PartitionSpec as P

NA = 256
NB = 256


def first_table(length):
    positions = jnp.arange(length, dtype=jnp.int32)
    angles = (positions[:, None] * positions[None, :] % length).astype(jnp.float32) * (
        2.0 * math.pi / length
    )
    cos_vals = jnp.cos(angles).astype(jnp.bfloat16)
    sin_vals = jnp.sin(angles).astype(jnp.bfloat16)
    first_half = jnp.stack([cos_vals, sin_vals], axis=1)
    second_half = jnp.stack([-sin_vals, cos_vals], axis=1)
    return jnp.stack([first_half, second_half], axis=0)


def second_table(length):
    positions = jnp.arange(length, dtype=jnp.int32)
    angles = (positions[:, None] * positions[None, :] % length).astype(jnp.float32) * (
        2.0 * math.pi / length
    )
    return jnp.stack([jnp.cos(angles), -jnp.sin(angles)], axis=1)


def first_pass(spectral, table):
    return lax.dot_general(
        spectral, table, (((0, 2), (0, 1)), ((), ())), preferred_element_type=jnp.float32
    )


def rotate(sectioned, bin_start):
    bin_index = bin_start + jnp.arange(sectioned.shape[1], dtype=jnp.int32)
    time_index = jnp.arange(sectioned.shape[3], dtype=jnp.int32)
    products = bin_index[:, None] * time_index[None, :] % (NA * NB)
    twist = products.astype(jnp.float32) * (2.0 * math.pi / (NA * NB))
    cos_vals = jnp.cos(twist)
    sin_vals = jnp.sin(twist)
    real_part = sectioned[:, :, 0] * cos_vals - sectioned[:, :, 1] * sin_vals
    imag_part = sectioned[:, :, 0] * sin_vals + sectioned[:, :, 1] * cos_vals
    return jnp.stack([real_part, imag_part], axis=2)


def second_pass(turned, table):
    return lax.dot_general(
        turned,
        table,
        (((1, 2), (0, 1)), ((), ())),
        precision=lax.Precision.HIGHEST,
        preferred_element_type=jnp.float32,
    )


def on_device(transfer, amplitudes, weights):
    weighted = weights[None, :, None] * amplitudes
    real_part = jnp.sum(
        transfer[0] * weighted[0][:, None, :] - transfer[1] * weighted[1][:, None, :], axis=0
    )
    imag_part = jnp.sum(
        transfer[0] * weighted[1][:, None, :] + transfer[1] * weighted[0][:, None, :], axis=0
    )
    partial_value = jnp.stack([real_part, imag_part])
    high_local = partial_value.shape[2] // NB
    table_one = first_table(NA)
    table_two = second_table(NB)
    freq_count = lax.axis_size("freq")
    summed = lax.psum_scatter(partial_value, "head", scatter_dimension=1, tiled=True)
    spectral = summed.astype(jnp.bfloat16).reshape(2, summed.shape[1], high_local, NB)
    narrow = NB // freq_count
    offset = lax.axis_index("freq") * narrow
    turned = rotate(
        first_pass(
            lax.all_to_all(spectral, "freq", split_axis=3, concat_axis=2, tiled=True), table_one
        ),
        offset,
    )
    return second_pass(
        lax.all_to_all(turned, "freq", split_axis=3, concat_axis=1, tiled=True), table_two
    )


def solution(mesh):
    in_specs = (P(None, "head", None, "freq"), P(None, "head", "freq"), P("head"))
    out_specs = P("head", "freq", None)
    return jax.shard_map(
        on_device, mesh=mesh, in_specs=in_specs, out_specs=out_specs, check_vma=False
    )
```

profile of v0, /device:TPU:0, one launch (start us, length us, event | category | flops | bytes accessed | tf_op | source)
XLA Modules:
  0.0 163.0 jit_solution(252775999542638760)
XLA Ops:
  0.0 1.0 copy_multiply_fusion
  1.0 10.1 %fusion.1 = (f32[256,2048]{1,0:T(8,128)S(1)}, f32[256,2048]{1,0:T(8,128)S(1)}) fusion(f32[9,2048]{1,0:T(8,128)S(1)} %get-tuple-element.10, f32[9,2048]{1,0:T(8,128)S(1)} %get-tuple-element.9, bf16[2,9,256,2048]{3,2,1,0:T(8,128)(2,1)} %param.3), kind=kLoop, calls=%fused_computation.5 | loop fusion | flops 46137344 | bytes 23216128 | tf_op jit(solution)/shard_map/reduce_sum | solution.py:62
  11.1 0.5 pad_maximum_fusion
  11.6 5.2 %copy.25 = f32[2,256,2048]{2,0,1:T(2,128)} copy(f32[2,256,2048]{2,1,0:T(8,128)S(1)} %pad_maximum_fusion) | data formatting | bytes 8388608 | tf_op jit(solution)/shard_map/stack | solution.py:68
  16.8 0.0 copy-start.1
  16.8 81.4 %all-reduce.2 = bf16[2,256,2048]{2,0,1:T(2,128)(2,1)S(1)} all-reduce(f32[2,256,2048]{2,0,1:T(2,128)} %copy.25), channel_id=2, replica_groups=mesh['head'=4,'freq'=32] {'head'}, use_global_device_ids=true, to_apply=%region_2.3.clone | all-reduce | flops 1048576 | bytes 6291456
  98.2 0.0 copy-done.1
  98.2 0.6 dynamic-slice
  99.5 0.4 dynamic-slice_convert_fusion
  99.9 0.3 reshape.161
  100.2 1.3 copy.26
  101.5 1.5 reshape.170
  103.0 8.0 %all-to-all-start = ((bf16[32,2,4096]{2,1,0:T(2,128)(2,1)}), bf16[32,2,4096]{2,1,0:T(2,128)(2,1)S(1)}, u32[]{:S(2)}, u32[]{:S(2)}) async-start(bf16[32,2,4096]{2,1,0:T(2,128)(2,1)} %reshape.170), calls=%async_computation | async-start | bytes 1048576 | tf_op jit(solution)/shard_map/all_to_all | solution.py:79
  111.0 1.0 fusion.19
  112.0 1.1 fusion.17
  113.2 0.1 fusion.27
  113.3 10.3 %all-to-all-done = bf16[32,2,4096]{2,1,0:T(2,128)(2,1)S(1)} async-done(((bf16[32,2,4096]{2,1,0:T(2,128)(2,1)}), bf16[32,2,4096]{2,1,0:T(2,128)(2,1)S(1)}, u32[]{:S(2)}, u32[]{:S(2)}) %all-to-all-start) | async-done | bytes 524320 | tf_op jit(solution)/shard_map/all_to_all | solution.py:79
  123.5 0.7 reshape.171
  124.2 0.3 copy.28
  124.5 1.2 copy.35
  125.7 0.4 convolution_bitcast_fusion
  126.1 0.1 multiply_subtract_fusion
  126.3 0.1 pad_maximum_fusion.1
  126.3 1.6 copy.31
  127.9 2.3 %reshape.172 = f32[32,1,8192]{2,1,0:T(1,128)} reshape(f32[256,2,8,64]{3,2,1,0:T(8,128)S(1)} %bitcast.51) | data formatting | bytes 2097152
  130.2 4.2 %all-to-all-start.1 = ((f32[32,1,8192]{2,1,0:T(1,128)}), f32[32,1,8192]{2,1,0:T(1,128)S(1)}, u32[]{:S(2)}, u32[]{:S(2)}) async-start(f32[32,1,8192]{2,1,0:T(1,128)} %reshape.172), calls=%async_computation.1 | async-start | bytes 2097152 | tf_op jit(solution)/shard_map/all_to_all | solution.py:84
  134.4 1.7 %fusion.15 = (f32[256,1,256]{2,0,1:T(8,128)S(1)}, f32[256,1,256]{2,0,1:T(8,128)}) fusion(), kind=kLoop, calls=%fused_computation.36 | loop fusion | flops 983040 | bytes 524288 | tf_op jit(solution)/shard_map/cos | solution.py:17
  136.1 15.4 %all-to-all-done.1 = f32[32,1,8192]{2,1,0:T(1,128)S(1)} async-done(((f32[32,1,8192]{2,1,0:T(1,128)}), f32[32,1,8192]{2,1,0:T(1,128)S(1)}, u32[]{:S(2)}, u32[]{:S(2)}) %all-to-all-start.1) | async-done | bytes 1048608 | tf_op jit(solution)/shard_map/all_to_all | solution.py:84
  151.5 0.5 broadcast.271
  152.0 3.2 %reduce = f32[32,8192]{1,0:T(8,128)S(1)} reduce(f32[32,1,8192]{2,1,0:T(1,128)S(1)} %all-to-all-done.1, f32[]{:T(128)} %broadcast.271), dimensions={1}, to_apply=%all_to_all.30.reduce_sub_computation | reduce | bytes 2097156 | tf_op jit(solution)/shard_map/all_to_all | solution.py:84
  155.2 0.8 reshape.173
  156.1 0.0 copy-start
  156.1 2.2 %copy.33 = f32[64,32,8,2,8]{0,4,3,2,1:T(8,128)} copy(f32[64,32,8,2,8]{0,2,3,4,1:T(8,128)S(1)} %bitcast.54) | data formatting | bytes 2097152 | tf_op jit(solution)/shard_map/all_to_all | solution.py:84
  158.3 2.9 %copy.34 = f32[64,256,2,8]{1,3,2,0:T(8,128)S(1)} copy(f32[64,256,2,8]{0,3,2,1:T(8,128)} %bitcast.55) | data formatting | bytes 2097152 | tf_op jit(solution)/shard_map/all_to_all | solution.py:84
  161.2 0.0 copy-done
  161.2 1.8 %convolution_bitcast_fusion.1 = f32[64,8,256]{2,1,0:T(8,128)} fusion(f32[64,256,2,8]{1,3,2,0:T(8,128)S(1)} %copy.34, f32[256,1,256]{2,0,1:T(8,128)S(1)} %copy-done, f32[256,1,256]{2,0,1:T(8,128)S(1)} %get-tuple-element.17), kind=kOutput, calls=%fused_computation.10 | convolution fusion | flops 805437440 | bytes 2097152 | tf_op jit(solution)/shard_map/dot_general | solution.py:51
  (3 shorter events, 0.1 us)
Async XLA Ops:
  16.8 81.5 %copy-start.1 = (u32[128]{0:T(128)S(1)}, u32[128]{0:T(128)}, u32[]{:S(2)}) copy-start(u32[128]{0:T(128)} %constant.49) | copy-start | bytes 1540
  103.0 20.5 %all-to-all-start = ((bf16[32,2,4096]{2,1,0:T(2,128)(2,1)}), bf16[32,2,4096]{2,1,0:T(2,128)(2,1)S(1)}, u32[]{:S(2)}, u32[]{:S(2)}) async-start(bf16[32,2,4096]{2,1,0:T(2,128)(2,1)} %reshape.170), calls=%async_computation | async-start | bytes 1048576 | tf_op jit(solution)/shard_map/all_to_all | solution.py:79
  130.2 21.3 %all-to-all-start.1 = ((f32[32,1,8192]{2,1,0:T(1,128)}), f32[32,1,8192]{2,1,0:T(1,128)S(1)}, u32[]{:S(2)}, u32[]{:S(2)}) async-start(f32[32,1,8192]{2,1,0:T(1,128)} %reshape.172), calls=%async_computation.1 | async-start | bytes 2097152 | tf_op jit(solution)/shard_map/all_to_all | solution.py:84
  156.1 5.1 %copy-start = (f32[256,1,256]{2,0,1:T(8,128)S(1)}, f32[256,1,256]{2,0,1:T(8,128)}, u32[]{:S(2)}) copy-start(f32[256,1,256]{2,0,1:T(8,128)} %get-tuple-element.18) | copy-start | bytes 786436
where the time goes:
time: 163 us
  blocking collectives  81.4 us (50%)
  waiting for transfers between devices  25.6 us (16%)
  local copies, waits for them, and re-layouts  21.8 us (13%)
  other arithmetic  19 us (12%)
  starting transfers between devices  12.1 us (7%)
  matrix products  2.22 us (1%)
    unnamed x1, blocking collectives  81.4 us
    all_to_all x1, waiting for transfers between devices, on_device(): lax.all_to_all(turned, 'freq', split_axis=3, concat_axis=1, tiled=True)  15.4 us
    all_to_all x1, waiting for transfers between devices, on_device(): lax.all_to_all(spectral, 'freq', split_axis=3, concat_axis=2, tiled=True)  10.3 us
    reduce_sum x1, other arithmetic, on_device(): jnp.sum(transfer[0] * weighted[0][:, None, :] - transfer[1] * weighted[1]...  10.1 us
    all_to_all x1, starting transfers between devices, on_device(): lax.all_to_all(spectral, 'freq', split_axis=3, concat_axis=2, tiled=True)  7.95 us
    unnamed x9, local copies, waits for them, and re-layouts  5.9 us
    all_to_all x3, local copies, waits for them, and re-layouts, on_device(): lax.all_to_all(turned, 'freq', split_axis=3, concat_axis=1, tiled=True)  5.66 us
    another operation x1, local copies, waits for them, and re-layouts, on_device(): partial_value = jnp.stack([real_part, imag_part])  5.17 us
  transfers between devices with their start and end apart: 2, of which 2 were waited for; matrix products, arithmetic and copies ran while one was open for 2% of the time, Pallas kernels for 0%

commit v1 on v0

v1 whole, which is shorter than its diff:
```python
import functools
import math

import jax
import jax.numpy as jnp
import ml_dtypes
import numpy as np
from jax import lax
from jax.experimental import pallas as pl
from jax.experimental.pallas import tpu as pltpu
from jax.sharding import PartitionSpec as P

N = 256
HALF = N // 2
HEADS = 9
SPOTS = 64
FREQ = 32
AL = 8
PL = 4
SLOTS = 8
MESH = pl.DeviceIdType.MESH


def tables():
    n = np.arange(N)
    angle = 2.0 * math.pi * ((n[:, None] * n[None, :]) % N) / N
    trig = np.stack([np.cos(angle), np.sin(angle)])
    trig = trig.reshape(2, N, FREQ, AL)
    first = np.zeros((2, 2, N, FREQ, 2, AL))
    for i in range(2):
        first[i, :, :, :, i, :] = trig
    first = first.reshape(4 * N, 2 * N).astype(ml_dtypes.bfloat16)
    order = np.zeros((2, HALF, HALF))
    order[0] = np.eye(HALF)
    order[1][np.arange(HALF), (HALF - np.arange(HALF)) % HALF] = 1.0
    order = order.astype(ml_dtypes.bfloat16)
    pairs = np.arange(HALF)
    mirror = np.where(pairs == 0, HALF, N - pairs)
    low = np.stack([pairs, mirror])
    turn = 2.0 * math.pi * ((low[:, :, None] * n) % (N * N)) / (N * N)
    cos_turn, sin_turn = np.cos(turn), np.sin(turn)
    cos_turn[1, 0], sin_turn[1, 0] = -np.sin(turn[1, 0]), np.cos(turn[1, 0])
    twist = np.stack([cos_turn, sin_turn], axis=2)
    twist = twist.reshape(2, FREQ, PL, 2, N).transpose(1, 4, 0, 2, 3).reshape(FREQ, N, 4 * PL)
    wide = np.zeros((FREQ, N, 128), np.float32)
    wide[:, :, : 4 * PL] = twist
    cos_two, sin_two = np.cos(angle)[:HALF], -np.sin(angle)[:HALF]
    sin_two[0] = -((-1.0) ** n)
    second = np.concatenate([cos_two, sin_two], axis=1).astype(np.float32)
    upper = second.astype(ml_dtypes.bfloat16)
    lower = (second - upper.astype(np.float32)).astype(ml_dtypes.bfloat16)
    second = np.concatenate([upper, lower], axis=0)
    return first, order, wide, second


def kernel(
    transfer, amplitudes, weights, first, order, twist, second,
    out,
    slabs, amp, wide, part, core_in, pair_out, pair_in, gather, bins_out, bins_in,
    first_v, order_v, twist_v, second_v, turn, passed, folded, fold_out, fold_in, fold_f32, staged,
    slab_sem, const_sem, core_send, core_recv, pair_send, pair_recv,
    bins_send, bins_recv, fold_send, fold_recv,
):
    head = lax.axis_index("head")
    me = lax.axis_index("freq")
    z, core = head // 2, lax.rem(head, 2)
    other_core = (z * 2 + 1 - core, me)
    other_z = ((1 - z) * 2 + core, me)
    f32, bf16 = jnp.float32, jnp.bfloat16

    def slab_copy(i):
        far, role, digit = i // 16, lax.rem(i // 8, 2), lax.rem(i, 8)
        half = jnp.where(far == 0, 1 - z, z)
        rows = pl.ds(pl.multiple_of(half * 128, 128), 128)
        lanes = pl.ds(pl.multiple_of(digit * N + role * HALF, 128), 128)
        slot = lax.rem(i, SLOTS)
        return pltpu.make_async_copy(
            transfer.at[:, :, rows, lanes], slabs.at[slot], slab_sem.at[slot]
        )

    consts = [
        pltpu.make_async_copy(amplitudes, amp, const_sem.at[0]),
        pltpu.make_async_copy(first, first_v, const_sem.at[1]),
        pltpu.make_async_copy(order, order_v, const_sem.at[2]),
        pltpu.make_async_copy(twist.at[me], twist_v, const_sem.at[3]),
        pltpu.make_async_copy(second, second_v, const_sem.at[4]),
    ]
    consts[0].start()

    @pl.loop(0, SLOTS)
    def _(i):
        slab_copy(i).start()

    barrier = pltpu.get_barrier_semaphore()

    @pl.loop(1, FREQ)
    def _(d):
        pl.semaphore_signal(
            barrier, inc=1, device_id=(head, lax.rem(me + d, FREQ)), device_id_type=MESH
        )

    pl.semaphore_signal(barrier, inc=1, device_id=other_core, device_id_type=MESH)
    pl.semaphore_signal(barrier, inc=1, device_id=other_z, device_id_type=MESH)

    consts[0].wait()
    for r in range(2):
        for h in range(HEADS):
            row = amp[r, h : h + 1, :] * weights[h]
            wide[r, h] = jnp.broadcast_to(row, (8, row.shape[1]))

    def add_headings(chunk):
        @pl.loop(0, 4)
        def _(s):
            i = chunk * 4 + s
            role, digit = lax.rem(i // 8, 2), lax.rem(i, 8)
            lanes = pl.ds(pl.multiple_of(digit * N + role * HALF, 128), 128)
            slot = lax.rem(i, SLOTS)
            slab_copy(i).wait()

            @pl.loop(0, 2)
            def _(mine):
                row = jnp.where(mine == 0, 1 - core, core) * SPOTS
                for tile in range(SPOTS // 16):
                    rows = pl.ds(pl.multiple_of(row + tile * 16, 16), 16)
                    real = imag = None
                    for h in range(HEADS):
                        tr = slabs[slot, 0, h, rows, :].astype(f32).reshape(2, 8, 128)
                        ti = slabs[slot, 1, h, rows, :].astype(f32).reshape(2, 8, 128)
                        wr = wide[0, h, :, lanes][None]
                        wi = wide[1, h, :, lanes][None]
                        re, im = tr * wr - ti * wi, tr * wi + ti * wr
                        real = re if real is None else real + re
                        imag = im if imag is None else imag + im
                    part[mine, chunk, s, tile * 16 : tile * 16 + 16, :] = real.reshape(16, 128)
                    part[mine, chunk, s, SPOTS + tile * 16 : SPOTS + tile * 16 + 16, :] = (
                        imag.reshape(16, 128)
                    )

            @pl.when(i + SLOTS < 32)
            def _():
                slab_copy(i + SLOTS).start()

    def core_copy(chunk):
        return pltpu.make_async_remote_copy(
            src_ref=part.at[0, chunk], dst_ref=core_in.at[chunk],
            send_sem=core_send.at[chunk], recv_sem=core_recv.at[chunk],
            device_id=other_core, device_id_type=MESH,
        )

    def pair_copy(chunk):
        return pltpu.make_async_remote_copy(
            src_ref=pair_out.at[chunk], dst_ref=pair_in.at[chunk],
            send_sem=pair_send.at[chunk], recv_sem=pair_recv.at[chunk],
            device_id=other_z, device_id_type=MESH,
        )

    def send_pair(chunk):
        core_copy(chunk).wait_recv()

        @pl.loop(0, 4)
        def _(s):
            pair_out[chunk, s] = (part[1, chunk, s] + core_in[chunk, s]).astype(bf16)

        pair_copy(chunk).start()

    for chunk in range(8):
        add_headings(chunk)
        if chunk == 0:
            pl.semaphore_wait(barrier, FREQ + 1)
        core_copy(chunk).start()
        if 1 <= chunk <= 4:
            send_pair(chunk - 1)
        if chunk == 4:
            for c in consts[1:]:
                c.start()

    for c in consts[1:]:
        c.wait()

    def send_bins(role):
        for half in range(2):
            chunk = role * 2 + half
            core_copy(4 + chunk).wait_recv()
            pair_copy(chunk).wait_recv()
            for s in range(4):
                value = part[1, 4 + chunk, s] + core_in[4 + chunk, s]
                value = (value + pair_in[chunk, s].astype(f32)).astype(bf16)
                moved = lax.dot_general(
                    order_v[role], value, (((1,), (1,)), ((), ())), preferred_element_type=f32
                )
                gather[role, pl.ds(half * 4 + s, HALF, stride=AL), :] = moved
        bins_out[role] = gather[role].reshape(FREQ, PL * AL, 128).astype(bf16)

        @pl.loop(1, FREQ)
        def _(d):
            to = lax.rem(me + d, FREQ)
            pltpu.make_async_remote_copy(
                src_ref=bins_out.at[role, to], dst_ref=bins_in.at[role, me],
                send_sem=bins_send.at[role], recv_sem=bins_recv.at[role],
                device_id=(head, to), device_id_type=MESH,
            ).start()

        bins_in[role, me] = bins_out[role, me]

    def all_but_one(ref, sem):
        return pltpu.make_async_copy(ref.at[pl.ds(0, FREQ - 1)], ref.at[pl.ds(0, FREQ - 1)], sem)

    send_bins(0)
    for i in range(4 * PL):
        turn[i] = jnp.broadcast_to(twist_v[:, i : i + 1], (N, 128))
    send_bins(1)

    lane = lax.broadcasted_iota(jnp.int32, (1, 128), 1)
    low = lane < SPOTS
    sign = jnp.where(low, -1.0, 1.0).astype(f32)
    lone = jnp.where(me == 0, 0.0, 1.0).astype(f32)
    ones = jnp.ones((1, 128), f32)
    scale = [
        [jnp.where(low, ones, lone)] + [ones] * (PL - 1),
        [jnp.where(low, lone, -ones)] + [-sign] * (PL - 1),
    ]

    for role in range(2):
        all_but_one(bins_in.at[role], bins_recv.at[role]).wait()
        both = jnp.concatenate(
            [bins_in[role, :, i * 16 : i * 16 + 16, :].reshape(2 * N, 128) for i in range(2)],
            axis=1,
        )
        for p2 in range(2):
            passed[...] = jnp.dot(
                first_v[p2 * 2 * N : (p2 + 1) * 2 * N, :], both, preferred_element_type=f32
            )
            for i in range(2):
                p = i * 2 + p2
                column = (role * PL + p) * 2

                @pl.loop(0, 4)
                def _(block):
                    rows = pl.ds(pl.multiple_of(block * 64, 64), 64)
                    more = pl.ds(pl.multiple_of(N + block * 64, 64), 64)
                    lanes = slice(i * 128, i * 128 + 128)
                    c, s = passed[rows, lanes], passed[more, lanes]
                    cw, sw = turn[column, rows, :], turn[column + 1, rows, :]
                    value = (c * cw - s * sw) + sign * pltpu.roll(s * cw + c * sw, SPOTS, 1)
                    value = (value * scale[role][p]).reshape(8, AL, 128)
                    times = pl.ds(pl.multiple_of(block * 8, 8), 8)
                    place = (times, slice(p * AL, (p + 1) * AL), slice(None))
                    if role == 0:
                        folded[place] = value
                    else:
                        folded[place] = folded[place] + value

    fold_out[...] = folded[...].astype(bf16)

    @pl.loop(1, FREQ)
    def _(d):
        to = lax.rem(me + d, FREQ)
        pltpu.make_async_remote_copy(
            src_ref=fold_out.at[to], dst_ref=fold_in.at[me],
            send_sem=fold_send.at[0], recv_sem=fold_recv.at[0],
            device_id=(head, to), device_id_type=MESH,
        ).start()

    fold_in[me] = fold_out[me]
    for chunk in range(8):
        core_copy(chunk).wait_send()
    for chunk in range(4):
        pair_copy(chunk).wait_send()
    for role in range(2):
        all_but_one(bins_out.at[role], bins_send.at[role]).wait()
    all_but_one(fold_in, fold_recv.at[0]).wait()

    fold_f32[...] = fold_in[...].astype(f32).reshape(FREQ * PL * AL, 128)
    for t in range(AL):
        value = fold_f32[pl.ds(t, HALF, stride=AL), :].astype(bf16)
        value = jnp.concatenate([value, value], axis=0)
        result = lax.dot_general(
            value, second_v[...], (((0,), (0,)), ((), ())), preferred_element_type=f32
        )
        result = result[:SPOTS, :N] + result[SPOTS:, N:]
        for i in range(2):
            staged[i, pl.ds(t, SPOTS, stride=AL), :] = result[:, i * 128 : i * 128 + 128]
    for i in range(2):
        out[:, i * 128 : i * 128 + 128] = staged[i]
    all_but_one(fold_out, fold_send.at[0]).wait()


def on_device(transfer, amplitudes, weights):
    f32, bf16 = jnp.float32, jnp.bfloat16
    any_spec = pl.BlockSpec(memory_space=pl.ANY)
    stress = pl.pallas_call(
        kernel,
        out_shape=jax.ShapeDtypeStruct((SPOTS * AL, N), f32),
        in_specs=[any_spec, any_spec, pl.BlockSpec(memory_space=pltpu.SMEM)] + [any_spec] * 4,
        out_specs=pl.BlockSpec(memory_space=pltpu.VMEM),
        scratch_shapes=[
            pltpu.VMEM((SLOTS, 2, HEADS, 128, 128), bf16),
            pltpu.VMEM((2, HEADS, AL * N), f32),
            pltpu.VMEM((2, HEADS, 8, AL * N), f32),
            pltpu.VMEM((2, 8, 4, 128, 128), f32),
            pltpu.VMEM((8, 4, 128, 128), f32),
            pltpu.VMEM((4, 4, 128, 128), bf16),
            pltpu.VMEM((4, 4, 128, 128), bf16),
            pltpu.VMEM((2, HALF * AL, 128), f32),
            pltpu.VMEM((2, FREQ, PL * AL, 128), bf16),
            pltpu.VMEM((2, FREQ, PL * AL, 128), bf16),
            pltpu.VMEM((4 * N, 2 * N), bf16),
            pltpu.VMEM((2, HALF, HALF), bf16),
            pltpu.VMEM((N, 128), f32),
            pltpu.VMEM((N, 2 * N), bf16),
            pltpu.VMEM((4 * PL, N, 128), f32),
            pltpu.VMEM((2 * N, N), f32),
            pltpu.VMEM((FREQ, PL * AL, 128), f32),
            pltpu.VMEM((FREQ, PL * AL, 128), bf16),
            pltpu.VMEM((FREQ, PL * AL, 128), bf16),
            pltpu.VMEM((FREQ * PL * AL, 128), f32),
            pltpu.VMEM((2, SPOTS * AL, 128), f32),
            pltpu.SemaphoreType.DMA((SLOTS,)),
            pltpu.SemaphoreType.DMA((5,)),
            pltpu.SemaphoreType.DMA((8,)),
            pltpu.SemaphoreType.DMA((8,)),
            pltpu.SemaphoreType.DMA((4,)),
            pltpu.SemaphoreType.DMA((4,)),
            pltpu.SemaphoreType.DMA((2,)),
            pltpu.SemaphoreType.DMA((2,)),
            pltpu.SemaphoreType.DMA((1,)),
            pltpu.SemaphoreType.DMA((1,)),
        ],
        compiler_params=pltpu.CompilerParams(
            collective_id=0, has_side_effects=True, vmem_limit_bytes=56 * 2**20
        ),
        cost_estimate=pl.CostEstimate(
            flops=900_000_000, bytes_accessed=22_000_000, transcendentals=0
        ),
    )(transfer, amplitudes, weights, *[jnp.asarray(table) for table in tables()])
    return stress.reshape(SPOTS, AL, N)


def solution(mesh):
    in_specs = (P(None, "head", None, "freq"), P(None, "head", "freq"), P("head"))
    out_specs = P("head", "freq", None)
    return jax.shard_map(
        on_device, mesh=mesh, in_specs=in_specs, out_specs=out_specs, check_vma=False
    )
```

time: 163 us -> 49.4 us (0.30)
  blocking collectives: 81.4 us -> 0 us
  Pallas kernels: 0 us -> 45.7 us
  waiting for transfers between devices: 25.6 us -> 0 us
  other arithmetic: 19 us -> 0 us
  local copies, waits for them, and re-layouts: 21.8 us -> 3.57 us
  starting transfers between devices: 12.1 us -> 0 us
  matrix products: 2.22 us -> 0 us
    unnamed x1 -> x0, blocking collectives: 81.4 us -> none
    pallas_call x0 -> x1, Pallas kernels: none -> 45.7 us  [on_device(): pl.pallas_call(kernel, out_shape=jax.ShapeDtypeStruct((SPOTS * AL, N), f3...]
    all_to_all x2 -> x0, waiting for transfers between devices: 25.6 us -> none  [the longest x1 15.4 us: on_device(): lax.all_to_all(turned, 'freq', split_axis=3, concat_axis=1, tiled=True)]
    all_to_all x2 -> x0, starting transfers between devices: 12.1 us -> none  [the longest x1 7.95 us: on_device(): lax.all_to_all(spectral, 'freq', split_axis=3, concat_axis=2, tiled=True)]
    reduce_sum x1 -> x0, other arithmetic: 10.1 us -> none  [on_device(): jnp.sum(transfer[0] * weighted[0][:, None, :] - transfer[1] * weighted[1]...]
    all_to_all x5 -> x0, local copies, waits for them, and re-layouts: 7.12 us -> none  [the longest x3 5.66 us: on_device(): lax.all_to_all(turned, 'freq', split_axis=3, concat_axis=1, tiled=True)]
    another operation x2 -> x0, local copies, waits for them, and re-layouts: 6.76 us -> none  [the longest x1 5.17 us: on_device(): partial_value = jnp.stack([real_part, imag_part])]
    all_to_all x1 -> x0, other arithmetic: 3.2 us -> none  [on_device(): lax.all_to_all(turned, 'freq', split_axis=3, concat_axis=1, tiled=True)]
  transfers between devices with their start and end apart: 2 -> 0, of which waited for: 2 -> 0; matrix products, arithmetic and copies ran while one was open for 2% -> 0% of each run, Pallas kernels for 0% -> 0%
where the time goes in v1:
time: 49.4 us; the launch traced here: 49.2 us
  Pallas kernels  45.7 us (93%)
  local copies, waits for them, and re-layouts  3.57 us (7%)
    pallas_call x1, Pallas kernels, on_device(): pl.pallas_call(kernel, out_shape=jax.ShapeDtypeStruct((SPOTS * AL, N), f3...  45.7 us
    unnamed x2, local copies, waits for them, and re-layouts  3.57 us

profile of v1, /device:TPU:0, one launch (start us, length us, event | category | flops | bytes accessed | tf_op | source)
XLA Modules:
  0.0 49.2 jit_solution(4153674784078464833)
XLA Ops:
  0.0 1.7 %copy.8.amplitudes = f32[2,9,2048]{2,1,0:T(8,128)} copy(f32[2,9,2048]{2,0,1:T(2,128)} %param.8) | data formatting | bytes 294912 | tf_op args[1]
  1.7 45.7 %shard_map.73 = f32[512,256]{1,0:T(8,128)} custom-call(bf16[2,9,256,2048]{3,2,1,0:T(8,128)(2,1)} %transfer.1, f32[2,9,2048]{2,1,0:T(8,128)} %copy.8.amplitudes, f32[9]{0:T(128)} %weights.1, bf16[1024,512]{1,0:T(8,128)(2,1)} %constant.8.clone.first, bf16[2,128,128]{2,1,0:T(8,128)(2,1)} %constant.9.clone.order, f32[32,256,128]{2,1,0:T(8,128)} %constant.10.clone.twist, ...), custom_call_target="tpu_custom_call" | custom-call | flops 900000000 | bytes 22000000 | tf_op jit(solution)/shard_map/pallas_call | solution.py:291
  47.4 1.9 %copy.10 = f32[64,8,256]{2,1,0:T(8,128)} copy(f32[64,8,256]{2,1,0:T(8,128)} %bitcast.1) | data formatting | bytes 1048576

commit v2 on v1

v2 whole, which is shorter than its diff:
```python
import functools
import math

import jax
import jax.numpy as jnp
import ml_dtypes
import numpy as np
from jax import lax
from jax.experimental import pallas as pl
from jax.experimental.pallas import tpu as pltpu
from jax.sharding import PartitionSpec as P

N = 256
HALF = N // 2
HEADS = 9
SPOTS = 64
FREQ = 32
AL = 8
PL = 4
EARLY = 2
LATE = PL - EARLY
SLOTS = 8
MESH = pl.DeviceIdType.MESH


def tables():
    n = np.arange(N)
    angle = 2.0 * math.pi * ((n[:, None] * n[None, :]) % N) / N
    trig = np.stack([np.cos(angle), np.sin(angle)])
    trig = trig.reshape(2, N, FREQ, AL)
    first = np.zeros((2, 2, N, FREQ, 2, AL))
    for i in range(2):
        first[i, :, :, :, i, :] = trig
    first = first.reshape(4 * N, 2 * N).astype(ml_dtypes.bfloat16)
    pairs = HALF // PL * np.arange(PL) + np.arange(FREQ)[:, None]
    rows = np.concatenate([pairs[:, :EARLY].reshape(-1), pairs[:, EARLY:].reshape(-1)])
    order = np.zeros((2, HALF, HALF))
    order[0][np.arange(HALF), rows] = 1.0
    order[1][np.arange(HALF), (HALF - rows) % HALF] = 1.0
    order = order.astype(ml_dtypes.bfloat16)
    pairs = pairs.reshape(-1)
    mirror = np.where(pairs == 0, HALF, N - pairs)
    low = np.stack([pairs, mirror])
    turn = 2.0 * math.pi * ((low[:, :, None] * n) % (N * N)) / (N * N)
    cos_turn, sin_turn = np.cos(turn), np.sin(turn)
    cos_turn[1, 0], sin_turn[1, 0] = -np.sin(turn[1, 0]), np.cos(turn[1, 0])
    twist = np.stack([cos_turn, sin_turn], axis=2)
    twist = twist.reshape(2, FREQ, PL, 2, N).transpose(1, 4, 0, 2, 3).reshape(FREQ, N, 4 * PL)
    wide = np.zeros((FREQ, N, 128), np.float32)
    wide[:, :, : 4 * PL] = twist
    cos_two, sin_two = np.cos(angle)[:HALF], -np.sin(angle)[:HALF]
    sin_two[0] = -((-1.0) ** n)
    second = np.concatenate([cos_two, sin_two], axis=1).astype(np.float32)[pairs]
    upper = second.astype(ml_dtypes.bfloat16)
    lower = (second - upper.astype(np.float32)).astype(ml_dtypes.bfloat16)
    second = np.concatenate([upper, lower], axis=0)
    return first, order, wide, second


def farthest_first():
    steps = [(y, x, z) for y in range(4) for x in range(4) for z in range(2)]
    return sorted(steps, key=lambda d: -(min(d[0], 4 - d[0]) + min(d[1], 4 - d[1]) + d[2]))[:-1]


def kernel(
    transfer, amplitudes, weights, first, order, twist,
    out,
    slabs, amp, wide, part, core_in, pair_out, pair_in, early_own, gather_early, gather_late,
    early_out, early_in, late_out, late_in,
    first_v, order_v, twist_v, turn, passed, folded, late_folded, cross_out, cross_in,
    fold_out, fold_in,
    slab_sem, const_sem, core_send, core_recv, pair_send, pair_recv,
    bins_send, bins_recv, cross_send, cross_recv, fold_send, fold_recv,
):
    head = lax.axis_index("head")
    me = lax.axis_index("freq")
    z, core = head // 2, lax.rem(head, 2)
    other_core = (z * 2 + 1 - core, me)
    other_z = ((1 - z) * 2 + core, me)
    f32, bf16 = jnp.float32, jnp.bfloat16
    y, x, z_low = me // 8, lax.rem(me // 2, 4), lax.rem(me, 2)
    others = [
        lax.rem(y + dy, 4) * 8 + lax.rem(x + dx, 4) * 2 + lax.rem(z_low + dz, 2)
        for dy, dx, dz in farthest_first()
    ]

    def slab_copy(i):
        far, role, digit = i // 16, lax.rem(i // 8, 2), lax.rem(i, 8)
        half = jnp.where(far == 0, 1 - z, z)
        rows = pl.ds(pl.multiple_of(half * 128, 128), 128)
        lanes = pl.ds(pl.multiple_of(digit * N + role * HALF, 128), 128)
        slot = lax.rem(i, SLOTS)
        return pltpu.make_async_copy(
            transfer.at[:, :, rows, lanes], slabs.at[slot], slab_sem.at[slot]
        )

    consts = [
        pltpu.make_async_copy(amplitudes, amp, const_sem.at[0]),
        pltpu.make_async_copy(order, order_v, const_sem.at[1]),
        pltpu.make_async_copy(first, first_v, const_sem.at[2]),
        pltpu.make_async_copy(twist.at[me], twist_v, const_sem.at[3]),
    ]
    consts[0].start()

    @pl.loop(0, SLOTS)
    def _(i):
        slab_copy(i).start()

    consts[1].start()
    barrier = pltpu.get_barrier_semaphore()
    pl.semaphore_signal(barrier, inc=1, device_id=other_z, device_id_type=MESH)
    pl.semaphore_signal(barrier, inc=1, device_id=other_core, device_id_type=MESH)
    for to in others:
        pl.semaphore_signal(barrier, inc=1, device_id=(head, to), device_id_type=MESH)

    consts[0].wait()
    for r in range(2):
        for h in range(HEADS):
            row = amp[h, r : r + 1, :] * weights[h]
            wide[r, h] = jnp.broadcast_to(row, (8, row.shape[1]))

    def add_headings(chunk):
        @pl.loop(0, 4)
        def _(s):
            i = chunk * 4 + s
            role, digit = lax.rem(i // 8, 2), lax.rem(i, 8)
            lanes = pl.ds(pl.multiple_of(digit * N + role * HALF, 128), 128)
            slot = lax.rem(i, SLOTS)
            slab_copy(i).wait()

            @pl.loop(0, 2)
            def _(mine):
                row = jnp.where(mine == 0, 1 - core, core) * SPOTS
                for tile in range(SPOTS // 16):
                    rows = pl.ds(pl.multiple_of(row + tile * 16, 16), 16)
                    real = imag = None
                    for h in range(HEADS):
                        tr = slabs[slot, 0, h, rows, :].astype(f32).reshape(2, 8, 128)
                        ti = slabs[slot, 1, h, rows, :].astype(f32).reshape(2, 8, 128)
                        wr = wide[0, h, :, lanes][None]
                        wi = wide[1, h, :, lanes][None]
                        re, im = tr * wr - ti * wi, tr * wi + ti * wr
                        real = re if real is None else real + re
                        imag = im if imag is None else imag + im
                    part[mine, chunk, s, tile * 16 : tile * 16 + 16, :] = real.reshape(16, 128)
                    part[mine, chunk, s, SPOTS + tile * 16 : SPOTS + tile * 16 + 16, :] = (
                        imag.reshape(16, 128)
                    )

            @pl.when(i + SLOTS < 32)
            def _():
                slab_copy(i + SLOTS).start()

    def core_copy(chunk):
        return pltpu.make_async_remote_copy(
            src_ref=part.at[0, chunk], dst_ref=core_in.at[chunk],
            send_sem=core_send.at[chunk], recv_sem=core_recv.at[chunk],
            device_id=other_core, device_id_type=MESH,
        )

    def pair_copy(chunk):
        return pltpu.make_async_remote_copy(
            src_ref=pair_out.at[chunk], dst_ref=pair_in.at[chunk],
            send_sem=pair_send.at[chunk], recv_sem=pair_recv.at[chunk],
            device_id=other_z, device_id_type=MESH,
        )

    def to_rows(table, value):
        return lax.dot_general(
            table, value, (((1,), (1,)), ((), ())), preferred_element_type=f32
        )

    def place(chunk, s, pairs):
        role, digit = chunk % 4 // 2, chunk % 2 * 4 + s
        return pl.ds(role * AL + digit, FREQ * pairs, stride=2 * AL)

    def chip_sum(chunk):
        core_copy(chunk).wait_recv()
        return (part[1, chunk] + core_in[chunk]).reshape(4 * 128, 128)

    def move_far(chunk):
        moved = to_rows(order_v[chunk // 2], chip_sum(chunk).astype(bf16))
        for s in range(4):
            slab = moved[:, s * 128 : s * 128 + 128]
            pair_out[chunk, s] = slab[: FREQ * EARLY].astype(bf16)
            gather_late[0, place(chunk, s, LATE), :] = slab[FREQ * EARLY :]
        pair_copy(chunk).start()

    def move_own(chunk):
        value = chip_sum(chunk)
        upper = value.astype(bf16)
        lower = (value - upper.astype(f32)).astype(bf16)
        role = (chunk - 4) // 2
        moved = to_rows(order_v[role], upper)
        rest = to_rows(order_v[role, : FREQ * EARLY], lower)
        for s in range(4):
            lanes = slice(s * 128, s * 128 + 128)
            early_own[chunk - 4, s] = moved[: FREQ * EARLY, lanes] + rest[:, lanes]
            gather_late[1, place(chunk, s, LATE), :] = moved[FREQ * EARLY :, lanes]

    def send_all(source, landing, send_sem, recv_sem):
        for to in others:
            pltpu.make_async_remote_copy(
                src_ref=source.at[to], dst_ref=landing.at[me],
                send_sem=send_sem, recv_sem=recv_sem,
                device_id=(head, to), device_id_type=MESH,
            ).start()
        landing[me] = source[me]

    def all_but_one(ref, sem):
        return pltpu.make_async_copy(ref.at[pl.ds(0, FREQ - 1)], ref.at[pl.ds(0, FREQ - 1)], sem)

    def send_late(group):
        late_out[group] = gather_late[group].reshape(FREQ, LATE * 2 * AL, 128).astype(bf16)
        send_all(late_out.at[group], late_in.at[group], bins_send.at[group], bins_recv.at[group])

    for chunk in range(8):
        add_headings(chunk)
        if chunk == 0:
            pl.semaphore_wait(barrier, FREQ + 1)
            consts[1].wait()
        core_copy(chunk).start()
        if 1 <= chunk <= 4:
            move_far(chunk - 1)
        if chunk == 4:
            send_late(0)
            for c in consts[2:]:
                c.start()
        if chunk > 4:
            move_own(chunk - 1)
    move_own(7)
    send_late(1)
    for c in consts[2:]:
        c.wait()
    for i in range(4 * PL):
        turn[i] = jnp.broadcast_to(twist_v[:, i : i + 1], (N, 128))

    for chunk in range(4):
        pair_copy(chunk).wait_recv()
        for s in range(4):
            gather_early[place(chunk, s, EARLY), :] = (
                early_own[chunk, s] + pair_in[chunk, s].astype(f32)
            )
    early_out[...] = gather_early[...].reshape(FREQ, EARLY * 2 * AL, 128).astype(bf16)
    send_all(early_out, early_in, bins_send.at[2], bins_recv.at[2])

    lane = lax.broadcasted_iota(jnp.int32, (1, 128), 1)
    low = lane < SPOTS
    sign = jnp.where(low, -1.0, 1.0).astype(f32)
    lone = jnp.where(me == 0, 0.0, 1.0).astype(f32)
    ones = jnp.ones((1, 128), f32)

    def first_pass(bins, pairs, store):
        count = len(pairs)
        both = jnp.concatenate(
            [bins[:, i * 16 : i * 16 + 16, :].reshape(2 * N, 128) for i in range(count)], axis=1
        )
        for role in range(2):
            passed[role, :, : count * 128] = jnp.dot(
                first_v[role * 2 * N : (role + 1) * 2 * N, :], both, preferred_element_type=f32
            )
        for i, p in enumerate(pairs):
            if p == 0:
                a, b = jnp.where(low, ones, lone), jnp.where(low, lone, -ones)
                a_far, b_far = jnp.where(low, lone, ones), jnp.where(low, -ones, lone)
            else:
                a, b, a_far, b_far = ones, -sign, ones, sign

            @pl.loop(0, 4)
            def _(block):
                rows = pl.ds(pl.multiple_of(block * 64, 64), 64)
                more = pl.ds(pl.multiple_of(N + block * 64, 64), 64)
                lanes = slice(i * 128, i * 128 + 128)
                straight, crossed = [], []
                for role in range(2):
                    c, s = passed[role, rows, lanes], passed[role, more, lanes]
                    column = (role * PL + p) * 2
                    cw, sw = turn[column, rows, :], turn[column + 1, rows, :]
                    straight.append(c * cw - s * sw)
                    crossed.append(s * cw + c * sw)
                value = a * straight[0] + b * straight[1]
                value += sign * pltpu.roll(a_far * crossed[0] + b_far * crossed[1], SPOTS, 1)
                store(i, pl.ds(pl.multiple_of(block * 8, 8), 8), value.reshape(8, AL, 128))

    def store_cross(i, times, value):
        late_folded[times, i * AL : i * AL + AL, :] = value

    def store_late(i, times, value):
        folded[times, (EARLY + i) * AL : (EARLY + i + 1) * AL, :] = value

    def store_early(i, times, value):
        folded[times, i * AL : i * AL + AL, :] = value

    late_pairs = list(range(EARLY, PL))
    all_but_one(late_in.at[0], bins_recv.at[0]).wait()
    first_pass(late_in.at[0], late_pairs, store_cross)
    cross_out[...] = late_folded[...].astype(bf16)
    cross = pltpu.make_async_remote_copy(
        src_ref=cross_out, dst_ref=cross_in, send_sem=cross_send.at[0],
        recv_sem=cross_recv.at[0], device_id=other_z, device_id_type=MESH,
    )
    cross.start()
    all_but_one(late_in.at[1], bins_recv.at[1]).wait()
    first_pass(late_in.at[1], late_pairs, store_late)
    all_but_one(early_in, bins_recv.at[2]).wait()
    first_pass(early_in, list(range(EARLY)), store_early)

    cross.wait_recv()
    fold_out[:, : EARLY * AL, :] = folded[:, : EARLY * AL, :].astype(bf16)
    fold_out[:, EARLY * AL :, :] = (
        folded[:, EARLY * AL :, :] + cross_in[...].astype(f32)
    ).astype(bf16)
    send_all(fold_out, fold_in, fold_send.at[0], fold_recv.at[0])

    for chunk in range(8):
        core_copy(chunk).wait_send()
    for chunk in range(4):
        pair_copy(chunk).wait_send()
    cross.wait_send()
    for group in range(2):
        all_but_one(late_out.at[group], bins_send.at[group]).wait()
    all_but_one(early_out, bins_send.at[2]).wait()
    all_but_one(fold_in, fold_recv.at[0]).wait()
    out[...] = fold_in[...]
    all_but_one(fold_out, fold_send.at[0]).wait()


def second_kernel(fold_in, second_v, out, fold_f32, staged):
    f32, bf16 = jnp.float32, jnp.bfloat16
    fold_f32[...] = fold_in[...].astype(f32).reshape(FREQ * PL * AL, 128)
    for t in range(AL):
        value = fold_f32[pl.ds(t, HALF, stride=AL), :].astype(bf16)
        value = jnp.concatenate([value, value], axis=0)
        result = lax.dot_general(
            value, second_v[...], (((0,), (0,)), ((), ())), preferred_element_type=f32
        )
        result = result[:SPOTS, :N] + result[SPOTS:, N:]
        for i in range(2):
            staged[i, pl.ds(t, SPOTS, stride=AL), :] = result[:, i * 128 : i * 128 + 128]
    for i in range(2):
        out[:, i * 128 : i * 128 + 128] = staged[i]


def on_device(transfer, amplitudes, weights):
    f32, bf16 = jnp.float32, jnp.bfloat16
    any_spec = pl.BlockSpec(memory_space=pl.ANY)
    first, order, twist, second = [jnp.asarray(table) for table in tables()]
    folded = pl.pallas_call(
        kernel,
        out_shape=jax.ShapeDtypeStruct((FREQ, PL * AL, 128), bf16),
        in_specs=[any_spec, any_spec, pl.BlockSpec(memory_space=pltpu.SMEM)] + [any_spec] * 3,
        out_specs=pl.BlockSpec(memory_space=pltpu.VMEM),
        scratch_shapes=[
            pltpu.VMEM((SLOTS, 2, HEADS, 128, 128), bf16),
            pltpu.VMEM((HEADS, 2, AL * N), f32),
            pltpu.VMEM((2, HEADS, 8, AL * N), f32),
            pltpu.VMEM((2, 8, 4, 128, 128), f32),
            pltpu.VMEM((8, 4, 128, 128), f32),
            pltpu.VMEM((4, 4, FREQ * EARLY, 128), bf16),
            pltpu.VMEM((4, 4, FREQ * EARLY, 128), bf16),
            pltpu.VMEM((4, 4, FREQ * EARLY, 128), f32),
            pltpu.VMEM((FREQ * EARLY * 2 * AL, 128), f32),
            pltpu.VMEM((2, FREQ * LATE * 2 * AL, 128), f32),
            pltpu.VMEM((FREQ, EARLY * 2 * AL, 128), bf16),
            pltpu.VMEM((FREQ, EARLY * 2 * AL, 128), bf16),
            pltpu.VMEM((2, FREQ, LATE * 2 * AL, 128), bf16),
            pltpu.VMEM((2, FREQ, LATE * 2 * AL, 128), bf16),
            pltpu.VMEM((4 * N, 2 * N), bf16),
            pltpu.VMEM((2, HALF, HALF), bf16),
            pltpu.VMEM((N, 128), f32),
            pltpu.VMEM((4 * PL, N, 128), f32),
            pltpu.VMEM((2, 2 * N, max(EARLY, LATE) * 128), f32),
            pltpu.VMEM((FREQ, PL * AL, 128), f32),
            pltpu.VMEM((FREQ, LATE * AL, 128), f32),
            pltpu.VMEM((FREQ, LATE * AL, 128), bf16),
            pltpu.VMEM((FREQ, LATE * AL, 128), bf16),
            pltpu.VMEM((FREQ, PL * AL, 128), bf16),
            pltpu.VMEM((FREQ, PL * AL, 128), bf16),
            pltpu.SemaphoreType.DMA((SLOTS,)),
            pltpu.SemaphoreType.DMA((4,)),
            pltpu.SemaphoreType.DMA((8,)),
            pltpu.SemaphoreType.DMA((8,)),
            pltpu.SemaphoreType.DMA((4,)),
            pltpu.SemaphoreType.DMA((4,)),
            pltpu.SemaphoreType.DMA((3,)),
            pltpu.SemaphoreType.DMA((3,)),
            pltpu.SemaphoreType.DMA((1,)),
            pltpu.SemaphoreType.DMA((1,)),
            pltpu.SemaphoreType.DMA((1,)),
            pltpu.SemaphoreType.DMA((1,)),
        ],
        compiler_params=pltpu.CompilerParams(
            collective_id=0, has_side_effects=True, vmem_limit_bytes=56 * 2**20
        ),
        cost_estimate=pl.CostEstimate(
            flops=900_000_000, bytes_accessed=22_000_000, transcendentals=0
        ),
    )(transfer, jnp.transpose(amplitudes, (1, 0, 2)), weights, first, order, twist)
    stress = pl.pallas_call(
        second_kernel,
        out_shape=jax.ShapeDtypeStruct((SPOTS * AL, N), f32),
        in_specs=[pl.BlockSpec(memory_space=pltpu.VMEM)] * 2,
        out_specs=pl.BlockSpec(memory_space=pltpu.VMEM),
        scratch_shapes=[
            pltpu.VMEM((FREQ * PL * AL, 128), f32),
            pltpu.VMEM((2, SPOTS * AL, 128), f32),
        ],
        cost_estimate=pl.CostEstimate(
            flops=270_000_000, bytes_accessed=1_000_000, transcendentals=0
        ),
    )(folded, second)
    return stress.reshape(SPOTS, AL, N)


def solution(mesh):
    in_specs = (P(None, "head", None, "freq"), P(None, "head", "freq"), P("head"))
    out_specs = P("head", "freq", None)
    return jax.shard_map(
        on_device, mesh=mesh, in_specs=in_specs, out_specs=out_specs, check_vma=False
    )
```

time: 49.4 us -> 42.5 us (0.86)
  Pallas kernels: 45.7 us -> 41.9 us
  local copies, waits for them, and re-layouts: 3.57 us -> 0 us
    pallas_call x1 -> x2, Pallas kernels: 45.7 us -> 41.9 us  [the longest x1 39.5 us: on_device(): pl.pallas_call(kernel, out_shape=jax.ShapeDtypeStruct((FREQ, PL * AL, 128...]
    unnamed x2 -> x0, local copies, waits for them, and re-layouts: 3.57 us -> none
where the time goes in v2:
time: 42.5 us; the launch traced here: 41.9 us
  Pallas kernels  41.9 us (99%)
    pallas_call x1, Pallas kernels, on_device(): pl.pallas_call(kernel, out_shape=jax.ShapeDtypeStruct((FREQ, PL * AL, 128...  39.5 us
    pallas_call x1, Pallas kernels, on_device(): pl.pallas_call(second_kernel, out_shape=jax.ShapeDtypeStruct((SPOTS * AL,...  2.37 us

profile of v2, /device:TPU:0, one launch (start us, length us, event | category | flops | bytes accessed | tf_op | source)
XLA Modules:
  0.0 41.9 jit_solution(6811979918336781056)
XLA Ops:
  0.0 39.5 %shard_map.73.fold_in = bf16[32,32,128]{2,1,0:T(8,128)(2,1)} custom-call(bf16[2,9,256,2048]{3,2,1,0:T(8,128)(2,1)} %transfer.1, f32[9,2,2048]{2,1,0:T(2,128)} %bitcast.2, f32[9]{0:T(128)} %weights.1, bf16[1024,512]{1,0:T(8,128)(2,1)} %constant.8.clone.first, bf16[2,128,128]{2,1,0:T(8,128)(2,1)} %constant.9.clone.order, f32[32,256,128]{2,1,0:T(8,128)} %constant.10.clone.twist), custom_call_target="tpu_custom_call" | custom-call | flops 900000000 | bytes 22000000 | tf_op jit(solution)/shard_map/pallas_call | solution.py:348
  39.5 2.4 %shard_map.74 = f32[512,256]{1,0:T(8,128)} custom-call(bf16[32,32,128]{2,1,0:T(8,128)(2,1)} %shard_map.73.fold_in, bf16[256,512]{1,0:T(8,128)(2,1)} %constant.11.clone.second_v), custom_call_target="tpu_custom_call" | custom-call | flops 270000000 | bytes 1000000 | tf_op jit(solution)/shard_map/pallas_call | solution.py:399

commit v3 on v2

--- a/solution.py
+++ b/solution.py
@@ -33,10 +33,9 @@
         first[i, :, :, :, i, :] = trig
     first = first.reshape(4 * N, 2 * N).astype(ml_dtypes.bfloat16)
     pairs = HALF // PL * np.arange(PL) + np.arange(FREQ)[:, None]
-    rows = np.concatenate([pairs[:, :EARLY].reshape(-1), pairs[:, EARLY:].reshape(-1)])
     order = np.zeros((2, HALF, HALF))
-    order[0][np.arange(HALF), rows] = 1.0
-    order[1][np.arange(HALF), (HALF - rows) % HALF] = 1.0
+    order[0] = np.eye(HALF)
+    order[1][np.arange(HALF), (HALF - np.arange(HALF)) % HALF] = 1.0
     order = order.astype(ml_dtypes.bfloat16)
     pairs = pairs.reshape(-1)
     mirror = np.where(pairs == 0, HALF, N - pairs)
@@ -64,11 +63,11 @@
 
 def kernel(
     transfer, amplitudes, weights, first, order, twist,
-    out,
-    slabs, amp, wide, part, core_in, pair_out, pair_in, early_own, gather_early, gather_late,
-    early_out, early_in, late_out, late_in,
-    first_v, order_v, twist_v, turn, passed, folded, late_folded, cross_out, cross_in,
-    fold_out, fold_in,
+    fold_in,
+    slabs, amp, wide, part, core_in, pair_out, pair_in, gather_own, gather_late,
+    own_out, own_in, late_out, late_in,
+    first_v, order_v, twist_v, turn, passed, folded, cross_out, cross_in,
+    fold_out,
     slab_sem, const_sem, core_send, core_recv, pair_send, pair_recv,
     bins_send, bins_recv, cross_send, cross_recv, fold_send, fold_recv,
 ):
@@ -131,21 +130,22 @@
             @pl.loop(0, 2)
             def _(mine):
                 row = jnp.where(mine == 0, 1 - core, core) * SPOTS
-                for tile in range(SPOTS // 16):
-                    rows = pl.ds(pl.multiple_of(row + tile * 16, 16), 16)
-                    real = imag = None
+                for first_tile in range(0, SPOTS // 16, 4):
+                    tiles = range(first_tile, first_tile + 4)
+                    sums = [[None, None] for _ in tiles]
                     for h in range(HEADS):
-                        tr = slabs[slot, 0, h, rows, :].astype(f32).reshape(2, 8, 128)
-                        ti = slabs[slot, 1, h, rows, :].astype(f32).reshape(2, 8, 128)
-                        wr = wide[0, h, :, lanes][None]
-                        wi = wide[1, h, :, lanes][None]
-                        re, im = tr * wr - ti * wi, tr * wi + ti * wr
-                        real = re if real is None else real + re
-                        imag = im if imag is None else imag + im
-                    part[mine, chunk, s, tile * 16 : tile * 16 + 16, :] = real.reshape(16, 128)
-                    part[mine, chunk, s, SPOTS + tile * 16 : SPOTS + tile * 16 + 16, :] = (
-                        imag.reshape(16, 128)
-                    )
+                        wr, wi = wide[0, h, :, lanes][None], wide[1, h, :, lanes][None]
+                        for k, tile in enumerate(tiles):
+                            rows = pl.ds(pl.multiple_of(row + tile * 16, 16), 16)
+                            tr = slabs[slot, 0, h, rows, :].astype(f32).reshape(2, 8, 128)
+                            ti = slabs[slot, 1, h, rows, :].astype(f32).reshape(2, 8, 128)
+                            re, im = tr * wr - ti * wi, tr * wi + ti * wr
+                            sums[k] = [re, im] if h == 0 else [sums[k][0] + re, sums[k][1] + im]
+                    for k, tile in enumerate(tiles):
+                        for c in range(2):
+                            part[mine, chunk, s, pl.ds(c * SPOTS + tile * 16, 16), :] = (
+                                sums[k][c].reshape(16, 128)
+                            )
 
             @pl.when(i + SLOTS < 32)
             def _():
@@ -170,33 +170,42 @@
             table, value, (((1,), (1,)), ((), ())), preferred_element_type=f32
         )
 
-    def place(chunk, s, pairs):
-        role, digit = chunk % 4 // 2, chunk % 2 * 4 + s
-        return pl.ds(role * AL + digit, FREQ * pairs, stride=2 * AL)
+    def digit_of(chunk, s):
+        return chunk % 2 * 4 + s
 
     def chip_sum(chunk):
         core_copy(chunk).wait_recv()
         return (part[1, chunk] + core_in[chunk]).reshape(4 * 128, 128)
 
     def move_far(chunk):
-        moved = to_rows(order_v[chunk // 2], chip_sum(chunk).astype(bf16))
+        role = chunk // 2
+        moved = to_rows(order_v[role], chip_sum(chunk).astype(bf16))
         for s in range(4):
             slab = moved[:, s * 128 : s * 128 + 128]
             pair_out[chunk, s] = slab[: FREQ * EARLY].astype(bf16)
-            gather_late[0, place(chunk, s, LATE), :] = slab[FREQ * EARLY :]
+            for i in range(LATE):
+                row = i * 2 * AL + role * AL + digit_of(chunk, s)
+                gather_late[pl.ds(row, FREQ, stride=LATE * 2 * AL), :] = slab[
+                    FREQ * (EARLY + i) : FREQ * (EARLY + i + 1)
+                ]
         pair_copy(chunk).start()
 
     def move_own(chunk):
-        value = chip_sum(chunk)
+        value = chip_sum(4 + chunk)
         upper = value.astype(bf16)
         lower = (value - upper.astype(f32)).astype(bf16)
-        role = (chunk - 4) // 2
+        role = chunk // 2
         moved = to_rows(order_v[role], upper)
         rest = to_rows(order_v[role, : FREQ * EARLY], lower)
+        pair_copy(chunk).wait_recv()
         for s in range(4):
             lanes = slice(s * 128, s * 128 + 128)
-            early_own[chunk - 4, s] = moved[: FREQ * EARLY, lanes] + rest[:, lanes]
-            gather_late[1, place(chunk, s, LATE), :] = moved[FREQ * EARLY :, lanes]
+            full = moved[: FREQ * EARLY, lanes] + rest[:, lanes] + pair_in[chunk, s].astype(f32)
+            for i in range(PL):
+                rows = slice(FREQ * i, FREQ * (i + 1))
+                gather_own[
+                    role, pl.ds(i * AL + digit_of(chunk, s), FREQ, stride=PL * AL), :
+                ] = full[rows] if i < EARLY else moved[rows, lanes]
 
     def send_all(source, landing, send_sem, recv_sem):
         for to in others:
@@ -210,9 +219,13 @@
     def all_but_one(ref, sem):
         return pltpu.make_async_copy(ref.at[pl.ds(0, FREQ - 1)], ref.at[pl.ds(0, FREQ - 1)], sem)
 
-    def send_late(group):
-        late_out[group] = gather_late[group].reshape(FREQ, LATE * 2 * AL, 128).astype(bf16)
-        send_all(late_out.at[group], late_in.at[group], bins_send.at[group], bins_recv.at[group])
+    def send_late():
+        late_out[...] = gather_late[...].reshape(FREQ, LATE * 2 * AL, 128).astype(bf16)
+        send_all(late_out, late_in, bins_send.at[2], bins_recv.at[2])
+
+    def send_own(role):
+        own_out[role] = gather_own[role].reshape(FREQ, PL * AL, 128).astype(bf16)
+        send_all(own_out.at[role], own_in.at[role], bins_send.at[role], bins_recv.at[role])
 
     for chunk in range(8):
         add_headings(chunk)
@@ -223,26 +236,18 @@
         if 1 <= chunk <= 4:
             move_far(chunk - 1)
         if chunk == 4:
-            send_late(0)
+            send_late()
             for c in consts[2:]:
                 c.start()
         if chunk > 4:
-            move_own(chunk - 1)
-    move_own(7)
-    send_late(1)
+            move_own(chunk - 5)
+    send_own(0)
+    move_own(3)
+    send_own(1)
     for c in consts[2:]:
         c.wait()
     for i in range(4 * PL):
         turn[i] = jnp.broadcast_to(twist_v[:, i : i + 1], (N, 128))
-
-    for chunk in range(4):
-        pair_copy(chunk).wait_recv()
-        for s in range(4):
-            gather_early[place(chunk, s, EARLY), :] = (
-                early_own[chunk, s] + pair_in[chunk, s].astype(f32)
-            )
-    early_out[...] = gather_early[...].reshape(FREQ, EARLY * 2 * AL, 128).astype(bf16)
-    send_all(early_out, early_in, bins_send.at[2], bins_recv.at[2])
 
     lane = lax.broadcasted_iota(jnp.int32, (1, 128), 1)
     low = lane < SPOTS
@@ -250,66 +255,81 @@
     lone = jnp.where(me == 0, 0.0, 1.0).astype(f32)
     ones = jnp.ones((1, 128), f32)
 
-    def first_pass(bins, pairs, store):
-        count = len(pairs)
+    def masks(p):
+        if p > 0:
+            return ones, -sign, ones, sign
+        return (
+            jnp.where(low, ones, lone), jnp.where(low, lone, -ones),
+            jnp.where(low, lone, ones), jnp.where(low, -ones, lone),
+        )
+
+    def first_pass(bins, count):
         both = jnp.concatenate(
             [bins[:, i * 16 : i * 16 + 16, :].reshape(2 * N, 128) for i in range(count)], axis=1
         )
-        for role in range(2):
-            passed[role, :, : count * 128] = jnp.dot(
-                first_v[role * 2 * N : (role + 1) * 2 * N, :], both, preferred_element_type=f32
+        for stream in range(2):
+            passed[stream, :, : count * 128] = jnp.dot(
+                first_v[stream * 2 * N : (stream + 1) * 2 * N, :], both, preferred_element_type=f32
             )
-        for i, p in enumerate(pairs):
-            if p == 0:
-                a, b = jnp.where(low, ones, lone), jnp.where(low, lone, -ones)
-                a_far, b_far = jnp.where(low, lone, ones), jnp.where(low, -ones, lone)
-            else:
-                a, b, a_far, b_far = ones, -sign, ones, sign
-
-            @pl.loop(0, 4)
-            def _(block):
-                rows = pl.ds(pl.multiple_of(block * 64, 64), 64)
-                more = pl.ds(pl.multiple_of(N + block * 64, 64), 64)
-                lanes = slice(i * 128, i * 128 + 128)
-                straight, crossed = [], []
-                for role in range(2):
-                    c, s = passed[role, rows, lanes], passed[role, more, lanes]
-                    column = (role * PL + p) * 2
-                    cw, sw = turn[column, rows, :], turn[column + 1, rows, :]
-                    straight.append(c * cw - s * sw)
-                    crossed.append(s * cw + c * sw)
-                value = a * straight[0] + b * straight[1]
-                value += sign * pltpu.roll(a_far * crossed[0] + b_far * crossed[1], SPOTS, 1)
-                store(i, pl.ds(pl.multiple_of(block * 8, 8), 8), value.reshape(8, AL, 128))
-
-    def store_cross(i, times, value):
-        late_folded[times, i * AL : i * AL + AL, :] = value
-
-    def store_late(i, times, value):
-        folded[times, (EARLY + i) * AL : (EARLY + i + 1) * AL, :] = value
-
-    def store_early(i, times, value):
-        folded[times, i * AL : i * AL + AL, :] = value
-
-    late_pairs = list(range(EARLY, PL))
-    all_but_one(late_in.at[0], bins_recv.at[0]).wait()
-    first_pass(late_in.at[0], late_pairs, store_cross)
-    cross_out[...] = late_folded[...].astype(bf16)
+
+    def twisted(stream, place, block, role, p):
+        rows = pl.ds(pl.multiple_of(block * 64, 64), 64)
+        more = pl.ds(pl.multiple_of(N + block * 64, 64), 64)
+        lanes = slice(place * 128, place * 128 + 128)
+        c, s = passed[stream, rows, lanes], passed[stream, more, lanes]
+        column = (role * PL + p) * 2
+        cw, sw = turn[column, rows, :], turn[column + 1, rows, :]
+        return c * cw - s * sw, s * cw + c * sw
+
+    def swap(value):
+        return sign * pltpu.roll(value, SPOTS, 1)
+
+    all_but_one(late_in, bins_recv.at[2]).wait()
+    first_pass(late_in, LATE)
+
+    @pl.loop(0, 4)
+    def _(block):
+        values = []
+        for i in range(LATE):
+            a, b, a_far, b_far = masks(EARLY + i)
+            straight, crossed = twisted(0, i, block, 0, EARLY + i)
+            straight_far, crossed_far = twisted(1, i, block, 1, EARLY + i)
+            value = a * straight + b * straight_far + swap(a_far * crossed + b_far * crossed_far)
+            values.append(value.reshape(8, AL, 128))
+        times = pl.ds(pl.multiple_of(block * 8, 8), 8)
+        cross_out[times] = jnp.concatenate(values, axis=1).astype(bf16)
+
     cross = pltpu.make_async_remote_copy(
         src_ref=cross_out, dst_ref=cross_in, send_sem=cross_send.at[0],
         recv_sem=cross_recv.at[0], device_id=other_z, device_id_type=MESH,
     )
     cross.start()
-    all_but_one(late_in.at[1], bins_recv.at[1]).wait()
-    first_pass(late_in.at[1], late_pairs, store_late)
-    all_but_one(early_in, bins_recv.at[2]).wait()
-    first_pass(early_in, list(range(EARLY)), store_early)
-
-    cross.wait_recv()
-    fold_out[:, : EARLY * AL, :] = folded[:, : EARLY * AL, :].astype(bf16)
-    fold_out[:, EARLY * AL :, :] = (
-        folded[:, EARLY * AL :, :] + cross_in[...].astype(f32)
-    ).astype(bf16)
+
+    for role in range(2):
+        all_but_one(own_in.at[role], bins_recv.at[role]).wait()
+        first_pass(own_in.at[role], 2)
+        for place in range(2):
+            if role == 1 and place == 1:
+                cross.wait_recv()
+
+            @pl.loop(0, 4)
+            def _(block):
+                values = []
+                for stream in range(2):
+                    p = place * 2 + stream
+                    straight, crossed = twisted(stream, place, block, role, p)
+                    values.append((masks(p)[role] * straight + swap(masks(p)[2 + role] * crossed)).reshape(8, AL, 128))
+                value = jnp.concatenate(values, axis=1)
+                times = pl.ds(pl.multiple_of(block * 8, 8), 8)
+                rows = slice(place * 16, place * 16 + 16)
+                if role == 0:
+                    folded[times, rows, :] = value
+                else:
+                    value += folded[times, rows, :]
+                    if place == 1:
+                        value += cross_in[times].astype(f32)
+                    fold_out[times, rows, :] = value.astype(bf16)
+
     send_all(fold_out, fold_in, fold_send.at[0], fold_recv.at[0])
 
     for chunk in range(8):
@@ -317,11 +337,10 @@
     for chunk in range(4):
         pair_copy(chunk).wait_send()
     cross.wait_send()
-    for group in range(2):
-        all_but_one(late_out.at[group], bins_send.at[group]).wait()
-    all_but_one(early_out, bins_send.at[2]).wait()
+    for role in range(2):
+        all_but_one(own_out.at[role], bins_send.at[role]).wait()
+    all_but_one(late_out, bins_send.at[2]).wait()
     all_but_one(fold_in, fold_recv.at[0]).wait()
-    out[...] = fold_in[...]
     all_but_one(fold_out, fold_send.at[0]).wait()
 
 
@@ -347,7 +366,7 @@
     first, order, twist, second = [jnp.asarray(table) for table in tables()]
     folded = pl.pallas_call(
         kernel,
-        out_shape=jax.ShapeDtypeStruct((FREQ, PL * AL, 128), bf16),
+        out_shape=pltpu.VMEM((FREQ, PL * AL, 128), bf16),
         in_specs=[any_spec, any_spec, pl.BlockSpec(memory_space=pltpu.SMEM)] + [any_spec] * 3,
         out_specs=pl.BlockSpec(memory_space=pltpu.VMEM),
         scratch_shapes=[
@@ -358,23 +377,20 @@
             pltpu.VMEM((8, 4, 128, 128), f32),
             pltpu.VMEM((4, 4, FREQ * EARLY, 128), bf16),
             pltpu.VMEM((4, 4, FREQ * EARLY, 128), bf16),
-            pltpu.VMEM((4, 4, FREQ * EARLY, 128), f32),
-            pltpu.VMEM((FREQ * EARLY * 2 * AL, 128), f32),
-            pltpu.VMEM((2, FREQ * LATE * 2 * AL, 128), f32),
-            pltpu.VMEM((FREQ, EARLY * 2 * AL, 128), bf16),
-            pltpu.VMEM((FREQ, EARLY * 2 * AL, 128), bf16),
-            pltpu.VMEM((2, FREQ, LATE * 2 * AL, 128), bf16),
-            pltpu.VMEM((2, FREQ, LATE * 2 * AL, 128), bf16),
+            pltpu.VMEM((2, FREQ * PL * AL, 128), f32),
+            pltpu.VMEM((FREQ * LATE * 2 * AL, 128), f32),
+            pltpu.VMEM((2, FREQ, PL * AL, 128), bf16),
+            pltpu.VMEM((2, FREQ, PL * AL, 128), bf16),
+            pltpu.VMEM((FREQ, LATE * 2 * AL, 128), bf16),
+            pltpu.VMEM((FREQ, LATE * 2 * AL, 128), bf16),
             pltpu.VMEM((4 * N, 2 * N), bf16),
             pltpu.VMEM((2, HALF, HALF), bf16),
             pltpu.VMEM((N, 128), f32),
             pltpu.VMEM((4 * PL, N, 128), f32),
-            pltpu.VMEM((2, 2 * N, max(EARLY, LATE) * 128), f32),
+            pltpu.VMEM((2, 2 * N, 2 * 128), f32),
             pltpu.VMEM((FREQ, PL * AL, 128), f32),
-            pltpu.VMEM((FREQ, LATE * AL, 128), f32),
             pltpu.VMEM((FREQ, LATE * AL, 128), bf16),
             pltpu.VMEM((FREQ, LATE * AL, 128), bf16),
-            pltpu.VMEM((FREQ, PL * AL, 128), bf16),
             pltpu.VMEM((FREQ, PL * AL, 128), bf16),
             pltpu.SemaphoreType.DMA((SLOTS,)),
             pltpu.SemaphoreType.DMA((4,)),
@@ -408,7 +424,7 @@
         cost_estimate=pl.CostEstimate(
             flops=270_000_000, bytes_accessed=1_000_000, transcendentals=0
         ),
-    )(folded, second)
+    )(pltpu.with_memory_space_constraint(folded, pltpu.VMEM), second)
     return stress.reshape(SPOTS, AL, N)
 
 

time: 42.5 us -> 41.2 us (0.969)
  Pallas kernels: 41.9 us -> 40.6 us
    pallas_call x1, Pallas kernels: 39.5 us -> 38.3 us  [on_device(): pl.pallas_call(kernel, out_shape=pltpu.VMEM((FREQ, PL * AL, 128), bf16),...]
where the time goes in v3:
time: 41.2 us; the launch traced here: 40.6 us
  Pallas kernels  40.6 us (99%)
    pallas_call x1, Pallas kernels, on_device(): pl.pallas_call(kernel, out_shape=pltpu.VMEM((FREQ, PL * AL, 128), bf16),...  38.3 us
    pallas_call x1, Pallas kernels, on_device(): pl.pallas_call(second_kernel, out_shape=jax.ShapeDtypeStruct((SPOTS * AL,...  2.3 us

profile of v3, /device:TPU:0, one launch (start us, length us, event | category | flops | bytes accessed | tf_op | source)
XLA Modules:
  0.0 40.6 jit_solution(9511450677165447649)
XLA Ops:
  0.0 38.3 %shard_map.73.fold_in = bf16[32,32,128]{2,1,0:T(8,128)(2,1)S(1)} custom-call(bf16[2,9,256,2048]{3,2,1,0:T(8,128)(2,1)} %transfer.1, f32[9,2,2048]{2,1,0:T(2,128)} %bitcast.2, f32[9]{0:T(128)} %weights.1, bf16[1024,512]{1,0:T(8,128)(2,1)} %constant.8.clone.first, bf16[2,128,128]{2,1,0:T(8,128)(2,1)} %constant.9.clone.order, f32[32,256,128]{2,1,0:T(8,128)} %constant.10.clone.twist), custom_call_target="tpu_custom_call" | custom-call | flops 900000000 | bytes 22000000 | tf_op jit(solution)/shard_map/pallas_call | solution.py:367
  38.3 2.3 %shard_map.74 = f32[512,256]{1,0:T(8,128)} custom-call(bf16[32,32,128]{2,1,0:T(8,128)(2,1)S(1)} %shard_map.73.fold_in, bf16[256,512]{1,0:T(8,128)(2,1)} %constant.11.clone.second_v), custom_call_target="tpu_custom_call" | custom-call | flops 270000000 | bytes 1000000 | tf_op jit(solution)/shard_map/pallas_call | solution.py:415

commit v4 on v3

--- a/solution.py
+++ b/solution.py
@@ -62,8 +62,8 @@
 
 
 def kernel(
-    transfer, amplitudes, weights, first, order, twist,
-    fold_in,
+    transfer, amplitudes, weights, first, order, twist, second,
+    fold_in, second_v,
     slabs, amp, wide, part, core_in, pair_out, pair_in, gather_own, gather_late,
     own_out, own_in, late_out, late_in,
     first_v, order_v, twist_v, turn, passed, folded, cross_out, cross_in,
@@ -98,8 +98,10 @@
         pltpu.make_async_copy(order, order_v, const_sem.at[1]),
         pltpu.make_async_copy(first, first_v, const_sem.at[2]),
         pltpu.make_async_copy(twist.at[me], twist_v, const_sem.at[3]),
+        pltpu.make_async_copy(second, second_v, const_sem.at[4]),
     ]
     consts[0].start()
+    consts[3].start()
 
     @pl.loop(0, SLOTS)
     def _(i):
@@ -117,6 +119,10 @@
         for h in range(HEADS):
             row = amp[h, r : r + 1, :] * weights[h]
             wide[r, h] = jnp.broadcast_to(row, (8, row.shape[1]))
+
+    consts[3].wait()
+    for i in range(4 * PL):
+        turn[i] = jnp.broadcast_to(twist_v[:, i : i + 1], (N, 128))
 
     def add_headings(chunk):
         @pl.loop(0, 4)
@@ -237,17 +243,15 @@
             move_far(chunk - 1)
         if chunk == 4:
             send_late()
-            for c in consts[2:]:
+            for c in (consts[2], consts[4]):
                 c.start()
         if chunk > 4:
             move_own(chunk - 5)
     send_own(0)
     move_own(3)
     send_own(1)
-    for c in consts[2:]:
+    for c in (consts[2], consts[4]):
         c.wait()
-    for i in range(4 * PL):
-        turn[i] = jnp.broadcast_to(twist_v[:, i : i + 1], (N, 128))
 
     lane = lax.broadcasted_iota(jnp.int32, (1, 128), 1)
     low = lane < SPOTS
@@ -344,31 +348,37 @@
     all_but_one(fold_out, fold_send.at[0]).wait()
 
 
-def second_kernel(fold_in, second_v, out, fold_f32, staged):
+def second_kernel(fold_in, second_v, out, fold_f32, staged, out_sem):
     f32, bf16 = jnp.float32, jnp.bfloat16
     fold_f32[...] = fold_in[...].astype(f32).reshape(FREQ * PL * AL, 128)
-    for t in range(AL):
-        value = fold_f32[pl.ds(t, HALF, stride=AL), :].astype(bf16)
-        value = jnp.concatenate([value, value], axis=0)
-        result = lax.dot_general(
-            value, second_v[...], (((0,), (0,)), ((), ())), preferred_element_type=f32
-        )
-        result = result[:SPOTS, :N] + result[SPOTS:, N:]
-        for i in range(2):
-            staged[i, pl.ds(t, SPOTS, stride=AL), :] = result[:, i * 128 : i * 128 + 128]
+    copies = []
     for i in range(2):
-        out[:, i * 128 : i * 128 + 128] = staged[i]
+        lanes = slice(i * 128, i * 128 + 128)
+        table = jnp.concatenate(
+            [second_v[:, lanes], second_v[:, N + i * 128 : N + i * 128 + 128]], axis=1
+        )
+        for t in range(AL):
+            value = fold_f32[pl.ds(t, HALF, stride=AL), :].astype(bf16)
+            value = jnp.concatenate([value, value], axis=0)
+            result = lax.dot_general(
+                value, table, (((0,), (0,)), ((), ())), preferred_element_type=f32
+            )
+            staged[i, pl.ds(t, SPOTS, stride=AL), :] = result[:SPOTS, :128] + result[SPOTS:, 128:]
+        copies.append(pltpu.make_async_copy(staged.at[i], out.at[:, lanes], out_sem.at[i]))
+        copies[-1].start()
+    for copy in copies:
+        copy.wait()
 
 
 def on_device(transfer, amplitudes, weights):
     f32, bf16 = jnp.float32, jnp.bfloat16
     any_spec = pl.BlockSpec(memory_space=pl.ANY)
     first, order, twist, second = [jnp.asarray(table) for table in tables()]
-    folded = pl.pallas_call(
+    folded, second = pl.pallas_call(
         kernel,
-        out_shape=pltpu.VMEM((FREQ, PL * AL, 128), bf16),
-        in_specs=[any_spec, any_spec, pl.BlockSpec(memory_space=pltpu.SMEM)] + [any_spec] * 3,
-        out_specs=pl.BlockSpec(memory_space=pltpu.VMEM),
+        out_shape=(pltpu.VMEM((FREQ, PL * AL, 128), bf16), pltpu.VMEM((N, 2 * N), bf16)),
+        in_specs=[any_spec, any_spec, pl.BlockSpec(memory_space=pltpu.SMEM)] + [any_spec] * 4,
+        out_specs=(pl.BlockSpec(memory_space=pltpu.VMEM),) * 2,
         scratch_shapes=[
             pltpu.VMEM((SLOTS, 2, HEADS, 128, 128), bf16),
             pltpu.VMEM((HEADS, 2, AL * N), f32),
@@ -393,7 +403,7 @@
             pltpu.VMEM((FREQ, LATE * AL, 128), bf16),
             pltpu.VMEM((FREQ, PL * AL, 128), bf16),
             pltpu.SemaphoreType.DMA((SLOTS,)),
-            pltpu.SemaphoreType.DMA((4,)),
+            pltpu.SemaphoreType.DMA((5,)),
             pltpu.SemaphoreType.DMA((8,)),
             pltpu.SemaphoreType.DMA((8,)),
             pltpu.SemaphoreType.DMA((4,)),
@@ -411,20 +421,21 @@
         cost_estimate=pl.CostEstimate(
             flops=900_000_000, bytes_accessed=22_000_000, transcendentals=0
         ),
-    )(transfer, jnp.transpose(amplitudes, (1, 0, 2)), weights, first, order, twist)
+    )(transfer, jnp.transpose(amplitudes, (1, 0, 2)), weights, first, order, twist, second)
     stress = pl.pallas_call(
         second_kernel,
         out_shape=jax.ShapeDtypeStruct((SPOTS * AL, N), f32),
         in_specs=[pl.BlockSpec(memory_space=pltpu.VMEM)] * 2,
-        out_specs=pl.BlockSpec(memory_space=pltpu.VMEM),
+        out_specs=any_spec,
         scratch_shapes=[
             pltpu.VMEM((FREQ * PL * AL, 128), f32),
             pltpu.VMEM((2, SPOTS * AL, 128), f32),
+            pltpu.SemaphoreType.DMA((2,)),
         ],
         cost_estimate=pl.CostEstimate(
             flops=270_000_000, bytes_accessed=1_000_000, transcendentals=0
         ),
-    )(pltpu.with_memory_space_constraint(folded, pltpu.VMEM), second)
+    )(*[pltpu.with_memory_space_constraint(v, pltpu.VMEM) for v in (folded, second)])
     return stress.reshape(SPOTS, AL, N)
 
 

time: 41.2 us -> 40.2 us (0.976)
  Pallas kernels: 40.6 us -> 39.7 us
    pallas_call x1, Pallas kernels: 2.3 us -> 1.24 us  [on_device(): pl.pallas_call(second_kernel, out_shape=jax.ShapeDtypeStruct((SPOTS * AL,...]
where the time goes in v4:
time: 40.2 us; the launch traced here: 39.7 us
  Pallas kernels  39.7 us (99%)
    pallas_call x1, Pallas kernels, on_device(): pl.pallas_call(kernel, out_shape=(pltpu.VMEM((FREQ, PL * AL, 128), bf16),...  38.4 us
    pallas_call x1, Pallas kernels, on_device(): pl.pallas_call(second_kernel, out_shape=jax.ShapeDtypeStruct((SPOTS * AL,...  1.24 us

profile of v4, /device:TPU:0, one launch (start us, length us, event | category | flops | bytes accessed | tf_op | source)
XLA Modules:
  0.0 39.7 jit_solution(7196518334199510158)
XLA Ops:
  0.0 38.4 %shard_map.73 = (bf16[32,32,128]{2,1,0:T(8,128)(2,1)S(1)}, bf16[256,512]{1,0:T(8,128)(2,1)S(1)}) custom-call(bf16[2,9,256,2048]{3,2,1,0:T(8,128)(2,1)} %transfer.1, f32[9,2,2048]{2,1,0:T(2,128)} %bitcast.2, f32[9]{0:T(128)} %weights.1, bf16[1024,512]{1,0:T(8,128)(2,1)} %constant.8.clone.first, bf16[2,128,128]{2,1,0:T(8,128)(2,1)} %constant.9.clone.order, ...), custom_call_target="tpu_custom_call" | custom-call | flops 900000000 | bytes 22000000 | tf_op jit(solution)/shard_map/pallas_call | solution.py:377
  38.5 1.2 %shard_map.74 = f32[512,256]{1,0:T(8,128)} custom-call(bf16[32,32,128]{2,1,0:T(8,128)(2,1)S(1)} %get-tuple-element.7.fold_in, bf16[256,512]{1,0:T(8,128)(2,1)S(1)} %get-tuple-element.8.second_v), custom_call_target="tpu_custom_call" | custom-call | flops 270000000 | bytes 1000000 | tf_op jit(solution)/shard_map/pallas_call | solution.py:425

commit v5 on v4

--- a/solution.py
+++ b/solution.py
@@ -133,7 +133,7 @@
             slot = lax.rem(i, SLOTS)
             slab_copy(i).wait()
 
-            @pl.loop(0, 2)
+            @pl.loop(0, 2, unroll=2)
             def _(mine):
                 row = jnp.where(mine == 0, 1 - core, core) * SPOTS
                 for first_tile in range(0, SPOTS // 16, 4):
@@ -291,7 +291,7 @@
     all_but_one(late_in, bins_recv.at[2]).wait()
     first_pass(late_in, LATE)
 
-    @pl.loop(0, 4)
+    @pl.loop(0, 4, unroll=2)
     def _(block):
         values = []
         for i in range(LATE):
@@ -316,7 +316,7 @@
             if role == 1 and place == 1:
                 cross.wait_recv()
 
-            @pl.loop(0, 4)
+            @pl.loop(0, 4, unroll=2)
             def _(block):
                 values = []
                 for stream in range(2):

time: 40.2 us -> 39.6 us (0.985)
  Pallas kernels: 39.7 us -> 39.1 us
    pallas_call x1, Pallas kernels: 38.4 us -> 37.9 us  [on_device(): pl.pallas_call(kernel, out_shape=(pltpu.VMEM((FREQ, PL * AL, 128), bf16),...]
where the time goes in v5:
time: 39.6 us; the launch traced here: 39.1 us
  Pallas kernels  39.1 us (99%)
    pallas_call x1, Pallas kernels, on_device(): pl.pallas_call(kernel, out_shape=(pltpu.VMEM((FREQ, PL * AL, 128), bf16),...  37.9 us
    pallas_call x1, Pallas kernels, on_device(): pl.pallas_call(second_kernel, out_shape=jax.ShapeDtypeStruct((SPOTS * AL,...  1.24 us

profile of v5, /device:TPU:0, one launch (start us, length us, event | category | flops | bytes accessed | tf_op | source)
XLA Modules:
  0.0 39.1 jit_solution(159101795034839495)
XLA Ops:
  0.0 37.9 %shard_map.73 = (bf16[32,32,128]{2,1,0:T(8,128)(2,1)S(1)}, bf16[256,512]{1,0:T(8,128)(2,1)S(1)}) custom-call(bf16[2,9,256,2048]{3,2,1,0:T(8,128)(2,1)} %transfer.1, f32[9,2,2048]{2,1,0:T(2,128)} %bitcast.2, f32[9]{0:T(128)} %weights.1, bf16[1024,512]{1,0:T(8,128)(2,1)} %constant.8.clone.first, bf16[2,128,128]{2,1,0:T(8,128)(2,1)} %constant.9.clone.order, ...), custom_call_target="tpu_custom_call" | custom-call | flops 900000000 | bytes 22000000 | tf_op jit(solution)/shard_map/pallas_call | solution.py:377
  37.9 1.2 %shard_map.74 = f32[512,256]{1,0:T(8,128)} custom-call(bf16[32,32,128]{2,1,0:T(8,128)(2,1)S(1)} %get-tuple-element.7.fold_in, bf16[256,512]{1,0:T(8,128)(2,1)S(1)} %get-tuple-element.8.second_v), custom_call_target="tpu_custom_call" | custom-call | flops 270000000 | bytes 1000000 | tf_op jit(solution)/shard_map/pallas_call | solution.py:425
